TPU v7x, 256 devices: a whole 4x4x8 slice. The times are simulated.
256 devices in a mesh: resp: 8 (over x, core), seq: 32 (over y, z).
Axes of the slice: x: 4, y: 4, z: 8, core: 2. Of those that a mesh axis runs over, the one named last changes fastest.
Arguments:
- queries: bfloat16 [8, 4096, 4096], P('resp', 'seq'), may hold values from -10 to 10
- resp_keys: bfloat16 [8, 4096, 512], P('resp', 'seq'), may hold values from -10 to 10
- response_values: bfloat16 [8, 4096, 512], P('resp', 'seq'), may hold values from -6 to 6
- prompt_keys: bfloat16 [2048, 512], P(('resp', 'seq')), may hold values from -10 to 10
- shared_prompt_values: bfloat16 [2048, 512], P(('resp', 'seq')), may hold values from -6 to 6
- value_head: float32 [4096], replicated, may hold values from -0.09375 to 0.09375
- token_ids: int32 [8, 4096], P('resp', 'seq'), may hold values from 0 to 128255
- policy_logprobs: float32 [8, 4096], P('resp', 'seq'), may hold values from -10 to -0.5
- ref_table: float32 [128256], replicated, may hold values from -10 to -0.5
- scores: float32 [8], P('resp'), may hold values from -4 to 4
- lengths: int32 [8], P('resp'), may hold values from 1 to 4096, 20480 in all
- horizon: float32 [8], P('resp'), may hold values from 40 to 16384
Outputs:
- attn_out: bfloat16 [8, 4096, 4096], P('resp', 'seq')
- values: float32 [8, 4096], P('resp', 'seq')
- advantages: float32 [8, 4096], P('resp', 'seq')
Inputs may be any that keep to these rules, and one draw needn't show every extreme that they name: `lengths`: each response's valid positions; the longest response fills all 4096.
All inputs are finite; a program needn't handle non-finite values. No bound on the sum of `lengths` on one device may be relied on, other than what follows from the above.
Results may differ from a plain program's by a relative error of at most 0.012.
Values may be sent and summed in bfloat16 or wider, within the bound.
A program may use at most 192 MiB of HBM per device.

v0:
```python
import functools
import math

import jax
import jax.numpy as jnp
from jax import lax
from jax.experimental import pallas as pl
from jax.experimental.pallas import tpu as pltpu
from jax.sharding import PartitionSpec as P

F32 = jnp.float32
BF16 = jnp.bfloat16
MESH = pl.DeviceIdType.MESH

HEADS = 4
GROUP = 8
D = 128
NX, NY, NZ = 4, 4, 8
ROWS = 128
STACK = GROUP * ROWS
PROMPT = 2048
REPLY = 4096
SUPER = NZ * ROWS
HALF = NZ // 2
CHUNK = 512
VOCAB = 128256
KL_BETA = 0.01
NEG = -1e30
SCALE = math.log2(math.e) / math.sqrt(D)


def fold(state, q, k, v, bias=None):
    peak, total, acc = state
    s = lax.dot_general(q, k, (((1,), (1,)), ((), ())), preferred_element_type=F32)
    if bias is not None:
        s = (s.reshape(GROUP, ROWS, CHUNK) + bias[None]).reshape(STACK, CHUNK)
    new = jnp.maximum(peak, jnp.max(s, axis=1, keepdims=True))
    scaled = new * SCALE
    w = jnp.exp2(s * SCALE - jnp.concatenate([scaled] * (CHUNK // D), axis=1))
    shrink = jnp.exp2(peak * SCALE - scaled)
    total = total * shrink + jnp.sum(w, axis=1, keepdims=True)
    acc = acc * shrink + jnp.dot(w.astype(BF16), v, preferred_element_type=F32)
    return new, total, acc


def stacked(qg, block):
    return jnp.concatenate([qg[block, :, j * D : (j + 1) * D] for j in range(GROUP)], axis=0)


def body(
    scores_ref, lengths_ref, horizon_ref, ids_smem, q_hbm, k_hbm, v_hbm, pk_ref, pv_ref, head_ref, ids_ref, logp_ref, table_hbm,
    attn_ref, values_ref, adv_ref,
    qg, kvg, pkv, pg, pk_all, pv_all, acc, peak, total, staged, past, causal, ob, og, table, picked, packet, packets,
    local_sem, qy_send, qy_recv, ky_send, ky_recv, py_send, py_recv, pz_send, pz_recv, px_send, px_recv,
    pc_send, pc_recv, ring_send, ring_recv, oy_send, oy_recv, gy_send, gy_recv, gz_send, gz_recv,
):
    r = lax.axis_index("resp")
    s = lax.axis_index("seq")
    x, c = r // 2, r % 2
    y, z = s // NZ, s % NZ
    ahead = lambda d: (r, lax.rem(y + d, NY) * NZ + z)
    along = lambda d: (r, y * NZ + lax.rem(z + d, NZ))
    across = lambda d: (lax.rem(x + d, NX) * 2 + c, s)
    twin = (x * 2 + (1 - c), s)

    def remote(src, dst, send, recv, device):
        copy = pltpu.make_async_remote_copy(
            src_ref=src, dst_ref=dst, send_sem=send, recv_sem=recv, device_id=device, device_id_type=MESH
        )
        copy.start()
        return copy

    def head_cols(h, width):
        return pl.ds(pl.multiple_of(h * width, width), width)

    own = [
        pltpu.make_async_copy(q_hbm.at[0, :, head_cols(y, STACK)], qg.at[y], local_sem.at[0]),
        pltpu.make_async_copy(k_hbm.at[0, :, head_cols(y, D)], kvg.at[0, y, z], local_sem.at[1]),
        pltpu.make_async_copy(v_hbm.at[0, :, head_cols(y, D)], kvg.at[1, y, z], local_sem.at[2]),
        pltpu.make_async_copy(table_hbm, table, local_sem.at[3]),
    ]
    for copy in own:
        copy.start()
    barrier = pltpu.get_barrier_semaphore()
    peers = [ahead(d) for d in range(1, NY)] + [along(d) for d in range(1, NZ)] + [across(d) for d in range(1, NX)] + [twin]
    for peer in peers:
        pl.semaphore_signal(barrier, inc=1, device_id=peer, device_id_type=MESH)

    for h in range(HEADS):
        cols = slice(h * D, (h + 1) * D)
        pkv[h] = jnp.concatenate([pk_ref[:, cols].astype(F32), pv_ref[:, cols].astype(F32)], axis=0).astype(BF16)
    pg[x, c, z, y] = pkv[y]

    order = [lax.rem(z + k + NZ, NZ) for k in (0, 1, -1, 2, -2, 3, -3, 4)]
    inside = lax.broadcasted_iota(jnp.int32, (ROWS, ROWS), 1) - lax.broadcasted_iota(jnp.int32, (ROWS, ROWS), 0)
    for k in range(NZ):
        causal[k // HALF, :, (k % HALF) * ROWS : (k % HALF + 1) * ROWS] = jnp.where(inside <= (z - order[k]) * ROWS, 0.0, NEG)

    own[3].wait()

    def pick(t, carry):
        row = ids_smem[0, t] // D
        picked[pl.ds(t, 1), :] = table[pl.ds(row, 1), :]
        return carry

    lax.fori_loop(0, ROWS, pick, 0)
    pl.semaphore_wait(barrier, len(peers))

    sent = []
    p_y, k_y, q_y = [], [], {}
    for d in range(1, NY):
        to = lax.rem(y + d, NY)
        p_y.append(remote(pkv.at[to], pg.at[x, c, z, y], py_send.at[d - 1], py_recv.at[d - 1], ahead(d)))
    for d in range(1, NY):
        to = lax.rem(y + d, NY)
        for i, src in enumerate((k_hbm, v_hbm)):
            k_y.append(
                remote(
                    src.at[0, :, head_cols(to, D)], kvg.at[i, y, z],
                    ky_send.at[d - 1, i], ky_recv.at[d - 1, i], ahead(d),
                )
            )
    for d in (1, 3, 2):
        to = lax.rem(y + d, NY)
        q_y[d] = remote(q_hbm.at[0, :, head_cols(to, STACK)], qg.at[y], qy_send.at[d - 1], qy_recv.at[d - 1], ahead(d))
    sent += p_y + k_y + list(q_y.values())

    for copy in p_y:
        copy.wait_recv()
    p_z = [remote(pg.at[x, c, z], pg.at[x, c, z], pz_send.at[d - 1], pz_recv.at[d - 1], along(d)) for d in range(1, NZ)]
    sent += p_z
    for copy in own[1:3]:
        copy.wait()
    for copy in k_y:
        copy.wait_recv()

    def ring_step(step):
        back = lax.rem(z - step + NZ, NZ)
        fore = lax.rem(z + step, NZ)
        if step < NZ // 2 - 1:
            parts = (kvg.at[:, :, back], kvg.at[:, :, fore])
        else:
            parts = (kvg.at[0, :, back], kvg.at[1, :, fore])
        out = [
            remote(parts[0], parts[0], ring_send.at[step, 0], ring_recv.at[step, 0], along(1)),
            remote(parts[1], parts[1], ring_send.at[step, 1], ring_recv.at[step, 1], along(NZ - 1)),
        ]
        sent.extend(out)
        return out

    ring = ring_step(0)
    for copy in p_z:
        copy.wait_recv()
    p_x = {d: remote(pg.at[x, c], pg.at[x, c], px_send.at[d - 1], px_recv.at[d - 1], across(d)) for d in (1, 3, 2)}
    p_c = {0: remote(pg.at[x, c], pg.at[x, c], pc_send.at[0], pc_recv.at[0], twin)}

    def pass_over(d):
        p_x[d].wait_recv()
        src = lax.rem(x - d + NX, NX)
        p_c[d] = remote(pg.at[src, c], pg.at[src, c], pc_send.at[d], pc_recv.at[d], twin)

    def unpack(i, d):
        p_c[d].wait_recv()
        both = pg[lax.rem(x - d + NX, NX)].astype(F32).reshape(2 * NZ * NY, 16, D)
        pk_all[i] = both[:, :8, :].reshape(CHUNK, D).astype(BF16)
        pv_all[i] = both[:, 8:, :].reshape(CHUNK, D).astype(BF16)

    def prompt_fold(i, d):
        block = lax.rem(y - d + NY, NY)
        if i == 0:
            if d == 0:
                own[0].wait()
            else:
                q_y[d].wait_recv()
            state = (jnp.full((STACK, D), NEG, F32), jnp.zeros((STACK, D), F32), jnp.zeros((STACK, D), F32))
        else:
            state = (peak[block], total[block], acc[block])
        peak[block], total[block], acc[block] = fold(state, stacked(qg, block), pk_all[i], pv_all[i])

    def ring_on(step):
        for copy in ring:
            copy.wait_recv()
        return ring_step(step)

    unpack(0, 0)
    prompt_fold(0, 0)
    pass_over(1)
    prompt_fold(0, 1)
    pass_over(3)
    prompt_fold(0, 3)
    ring = ring_on(1)
    pass_over(2)
    unpack(1, 1)
    for d in (0, 1, 3):
        prompt_fold(1, d)
    unpack(2, 3)
    prompt_fold(2, 0)
    ring = ring_on(2)
    for d in (1, 3):
        prompt_fold(2, d)
    for i in range(3):
        prompt_fold(i, 2)
    ring = ring_on(3)
    unpack(3, 2)
    for d in (0, 1, 3, 2):
        prompt_fold(3, d)
    sent += list(p_x.values()) + list(p_c.values())

    length = lengths_ref[0]
    lanes = lax.broadcasted_iota(jnp.int32, (1, ROWS), 1)

    def turn(t):
        return lax.rem(2 + 3 * t + 3 * (t * (t - 1) // 2), NY)

    def reply_half(half):
        for sup in range(NY):
            for k in range(HALF):
                rows = slice(k * ROWS, (k + 1) * ROWS)
                zz = order[half * HALF + k]
                staged[0, sup, rows] = kvg[0, sup, zz]
                staged[1, sup, rows] = kvg[1, sup, zz]
                past[sup, :, rows] = jnp.where(sup * SUPER + zz * ROWS + lanes < length, 0.0, NEG)

        def run(block):
            q = stacked(qg, block)
            state = (peak[block], total[block], acc[block])
            for sup in range(block):
                state = fold(state, q, staged[0, sup], staged[1, sup], past[sup])
            state = fold(state, q, staged[0, block], staged[1, block], causal[half] + past[block])
            peak[block], total[block], acc[block] = state

        def step(t, carry):
            d = turn(t)
            block = lax.rem(y + d, NY)
            lax.switch(block, [functools.partial(run, b) for b in range(NY)])
            if half == 1:
                out = (acc[block] / total[block]).astype(BF16)
                for j in range(GROUP):
                    ob[t, :, j * D : (j + 1) * D] = out[j * ROWS : (j + 1) * ROWS]

                @pl.when(t < NY - 1)
                def _():
                    home(t).start()

            return carry

        lax.fori_loop(0, NY, step, 0)

    def home(t):
        return pltpu.make_async_remote_copy(
            src_ref=ob.at[t], dst_ref=og.at[y], send_sem=oy_send.at[t], recv_sem=oy_recv.at[t],
            device_id=ahead(turn(t)), device_id_type=MESH,
        )

    reply_half(0)
    for copy in ring:
        copy.wait_recv()
    reply_half(1)
    og[y] = ob[NY - 1]
    o_y = [home(t) for t in range(NY - 1)]
    sent += o_y
    for copy in o_y:
        copy.wait_recv()
    back_home = [
        pltpu.make_async_copy(og.at[h], attn_ref.at[0, :, h * STACK : (h + 1) * STACK], local_sem.at[4 + h])
        for h in range(HEADS)
    ]
    for copy in back_home:
        copy.start()

    value = jnp.zeros((ROWS, 1), F32)
    for h in range(HEADS):
        value = value + jnp.sum(og[h].astype(F32) * head_ref[:, h * STACK : (h + 1) * STACK], axis=1, keepdims=True)
    sub = lax.broadcasted_iota(jnp.int32, (ROWS, ROWS), 0)
    lane = lax.broadcasted_iota(jnp.int32, (ROWS, ROWS), 1)
    as_row = lambda column, shift=0: jnp.sum(jnp.where(sub == lane + shift, column, 0.0), axis=0, keepdims=True)
    as_column = lambda row: jnp.sum(jnp.where(sub == lane, row, 0), axis=1, keepdims=True)
    place = s * ROWS + lax.broadcasted_iota(jnp.int32, (1, ROWS), 1)
    live = place < length
    value = jnp.where(s * ROWS + lax.broadcasted_iota(jnp.int32, (ROWS, 1), 0) < length, value, 0.0)
    value_row = as_row(value)
    values_ref[...] = value_row
    spot = as_column(ids_ref[...] % D)
    reference = as_row(jnp.sum(jnp.where(lane == spot, picked[...], 0.0), axis=1, keepdims=True))
    rewards = jnp.where(live, -KL_BETA * (logp_ref[...] - reference), 0.0)
    rewards = rewards + jnp.where(place == length - 1, scores_ref[0], 0.0)
    deltas = jnp.where(live, rewards + as_row(value, 1) - value_row, 0.0)
    rate = -1.0 / jnp.full((1, 1), horizon_ref[0], F32)
    gap = (lane - sub).astype(F32)
    decay = jnp.where(gap >= 0.0, jnp.exp(jnp.maximum(gap, 0.0) * rate), 0.0)
    local_adv = as_row(jnp.sum(decay * deltas, axis=1, keepdims=True))
    first = lax.broadcasted_iota(jnp.int32, (8, ROWS), 1)
    packet[...] = jnp.where(first == 0, local_adv[:, :1], jnp.where(first == 1, value_row[:, :1], 0.0))
    packets[z, y] = packet[...]

    g_y = [remote(packet, packets.at[z, y], gy_send.at[d - 1], gy_recv.at[d - 1], ahead(d)) for d in range(1, NY)]
    for copy in g_y:
        copy.wait_recv()
    g_z = [remote(packets.at[z], packets.at[z], gz_send.at[d - 1], gz_recv.at[d - 1], along(d)) for d in range(1, NZ)]
    for copy in g_z:
        copy.wait_recv()
    sent += g_y + g_z

    carry = jnp.zeros((1, 1), F32)
    beyond = jnp.zeros((1, 1), F32)
    for yy in range(NY):
        rows = packets[:, yy, 0, :]
        far = (yy * NZ + lax.broadcasted_iota(jnp.int32, (NZ, 1), 0) - s - 1).astype(F32)
        adv_weight = jnp.where(far >= 0.0, jnp.exp(jnp.maximum(far, 0.0) * ROWS * rate), 0.0)
        value_weight = jnp.where(far >= 1.0, jnp.exp((jnp.maximum(far - 1.0, 0.0) * ROWS + (ROWS - 1)) * rate), 0.0)
        carry = carry + jnp.sum(adv_weight * rows[:, :1] + value_weight * rows[:, 1:2], axis=0, keepdims=True)
        beyond = beyond + jnp.sum(jnp.where(far == 0.0, rows[:, 1:2], 0.0), axis=0, keepdims=True)
    along_row = lax.broadcasted_iota(jnp.int32, (1, ROWS), 1).astype(F32)
    tail = jnp.exp((ROWS - 1 - along_row) * rate) * beyond + jnp.exp((ROWS - along_row) * rate) * carry
    adv_ref[...] = jnp.where(live, local_adv + tail, 0.0)

    for copy in back_home:
        copy.wait()
    for copy in sent:
        copy.wait_send()


def local(queries, resp_keys, response_values, prompt_keys, prompt_values, value_head, token_ids, logprobs, ref_table, scores, lengths, horizon):
    smem = pl.BlockSpec(memory_space=pltpu.SMEM)
    vmem = pl.BlockSpec(memory_space=pltpu.VMEM)
    hbm = pl.BlockSpec(memory_space=pl.ANY)
    dma = pltpu.SemaphoreType.DMA
    return pl.pallas_call(
        body,
        out_shape=(
            jax.ShapeDtypeStruct((1, ROWS, HEADS * STACK), BF16),
            jax.ShapeDtypeStruct((1, ROWS), F32),
            jax.ShapeDtypeStruct((1, ROWS), F32),
        ),
        in_specs=[smem, smem, smem, smem, hbm, hbm, hbm, vmem, vmem, vmem, vmem, vmem, hbm],
        out_specs=(hbm, vmem, vmem),
        scratch_shapes=[
            pltpu.VMEM((NY, ROWS, STACK), BF16),
            pltpu.VMEM((2, NY, NZ, ROWS, D), BF16),
            pltpu.VMEM((HEADS, 16, D), BF16),
            pltpu.VMEM((NX, 2, NZ, NY, 16, D), BF16),
            pltpu.VMEM((PROMPT // CHUNK, CHUNK, D), BF16),
            pltpu.VMEM((PROMPT // CHUNK, CHUNK, D), BF16),
            pltpu.VMEM((NY, STACK, D), F32),
            pltpu.VMEM((NY, STACK, D), F32),
            pltpu.VMEM((NY, STACK, D), F32),
            pltpu.VMEM((2, NY, CHUNK, D), BF16),
            pltpu.VMEM((NY, 1, CHUNK), F32),
            pltpu.VMEM((2, ROWS, CHUNK), F32),
            pltpu.VMEM((NY, ROWS, STACK), BF16),
            pltpu.VMEM((HEADS, ROWS, STACK), BF16),
            pltpu.VMEM((VOCAB // D, D), F32),
            pltpu.VMEM((ROWS, D), F32),
            pltpu.VMEM((8, ROWS), F32),
            pltpu.VMEM((NZ, NY, 8, ROWS), F32),
            dma((8,)),
            dma((NY - 1,)), dma((NY - 1,)),
            dma((NY - 1, 2)), dma((NY - 1, 2)),
            dma((NY - 1,)), dma((NY - 1,)),
            dma((NZ - 1,)), dma((NZ - 1,)),
            dma((NX - 1,)), dma((NX - 1,)),
            dma((NX,)), dma((NX,)),
            dma((NZ // 2, 2)), dma((NZ // 2, 2)),
            dma((NY - 1,)), dma((NY - 1,)),
            dma((NY - 1,)), dma((NY - 1,)),
            dma((NZ - 1,)), dma((NZ - 1,)),
        ],
        compiler_params=pltpu.CompilerParams(
            collective_id=0, has_side_effects=True, vmem_limit_bytes=56 * 2**20
        ),
    )(
        scores, lengths, horizon, token_ids, queries, resp_keys, response_values, prompt_keys, prompt_values,
        value_head.reshape(1, HEADS * STACK), token_ids, logprobs, ref_table.reshape(VOCAB // D, D),
    )


def solution(mesh):
    return jax.shard_map(
        local,
        mesh=mesh,
        in_specs=(
            P("resp", "seq", None),
            P("resp", "seq", None),
            P("resp", "seq", None),
            P(("resp", "seq"), None),
            P(("resp", "seq"), None),
            P(),
            P("resp", "seq"),
            P("resp", "seq"),
            P(),
            P("resp"),
            P("resp"),
            P("resp"),
        ),
        out_specs=(P("resp", "seq", None), P("resp", "seq"), P("resp", "seq")),
        check_vma=False,
    )
```

profile of v0, /device:TPU:8, one launch (start us, length us, event | category | flops | bytes accessed | tf_op | source)
XLA Modules:
  0.0 84.8 jit_solution(13166093179862432860)
XLA Ops:
  2.6 78.9 %shard_map.139 = (bf16[1,128,4096]{2,1,0:T(8,128)(2,1)}, f32[1,128]{1,0:T(1,128)}, f32[1,128]{1,0:T(1,128)}) custom-call(f32[1]{0:T(128)S(6)} %copy.18.scores_ref, s32[1]{0:T(128)S(6)} %copy.19.lengths_ref, f32[1]{0:T(128)S(6)} %copy.20.horizon_ref, s32[1,128]{1,0:T(1,128)} %ids_ref.1, bf16[1,128,4096]{2,1,0:T(8,128)(2,1)} %q_hbm.1, ...), custom_call_target="tpu_custom_call" | custom-call | tf_op jit(solution)/shard_map/pallas_call | solution.py:328
  81.4 0.0 copy-start.1
  81.5 2.3 %copy.21 = bf16[1,128,4096]{2,1,0:T(8,128)(2,1)} copy(bf16[1,128,4096]{2,1,0:T(8,128)(2,1)} %get-tuple-element.6) | data formatting | bytes 2097152
  83.7 0.0 copy-done.1
  83.7 0.0 copy-start
  83.7 0.5 copy.22
  84.3 0.1 copy-done
  84.3 0.5 copy.23
Async XLA Ops:
  81.4 2.3 %copy-start.1 = (f32[1,128]{1,0:T(1,128)S(1)}, f32[1,128]{1,0:T(1,128)}, u32[]{:S(2)}) copy-start(f32[1,128]{1,0:T(1,128)} %get-tuple-element.7) | copy-start | bytes 1540
  83.7 0.6 copy-start
where the time goes:
time: 85.8 us; the launch traced here: 84.8 us
  Pallas kernels  78.9 us (92%)
  local copies, waits for them, and re-layouts  3.38 us (4%)
  between operations  2.59 us (3%)
    pallas_call x1, Pallas kernels, local(): pl.pallas_call(body, out_shape=(jax.ShapeDtypeStruct((1, ROWS, HEADS * ST...  78.9 us
    unnamed x7, local copies, waits for them, and re-layouts  3.38 us

commit v1 on v0

--- a/solution.py
+++ b/solution.py
@@ -16,6 +16,7 @@
 GROUP = 8
 D = 128
 NX, NY, NZ = 4, 4, 8
+SEQ = NY * NZ
 ROWS = 128
 STACK = GROUP * ROWS
 PROMPT = 2048
@@ -23,6 +24,8 @@
 SUPER = NZ * ROWS
 HALF = NZ // 2
 CHUNK = 512
+SHARE = 256
+WING = STACK // 2
 VOCAB = 128256
 KL_BETA = 0.01
 NEG = -1e30
@@ -33,10 +36,10 @@
     peak, total, acc = state
     s = lax.dot_general(q, k, (((1,), (1,)), ((), ())), preferred_element_type=F32)
     if bias is not None:
-        s = (s.reshape(GROUP, ROWS, CHUNK) + bias[None]).reshape(STACK, CHUNK)
+        s = (s.reshape(GROUP, ROWS, -1) + bias[None]).reshape(s.shape)
     new = jnp.maximum(peak, jnp.max(s, axis=1, keepdims=True))
     scaled = new * SCALE
-    w = jnp.exp2(s * SCALE - jnp.concatenate([scaled] * (CHUNK // D), axis=1))
+    w = jnp.exp2(s * SCALE - jnp.concatenate([scaled] * (s.shape[1] // D), axis=1))
     shrink = jnp.exp2(peak * SCALE - scaled)
     total = total * shrink + jnp.sum(w, axis=1, keepdims=True)
     acc = acc * shrink + jnp.dot(w.astype(BF16), v, preferred_element_type=F32)
@@ -51,8 +54,8 @@
     scores_ref, lengths_ref, horizon_ref, ids_smem, q_hbm, k_hbm, v_hbm, pk_ref, pv_ref, head_ref, ids_ref, logp_ref, table_hbm,
     attn_ref, values_ref, adv_ref,
     qg, kvg, pkv, pg, pk_all, pv_all, acc, peak, total, staged, past, causal, ob, og, table, picked, packet, packets,
-    local_sem, qy_send, qy_recv, ky_send, ky_recv, py_send, py_recv, pz_send, pz_recv, px_send, px_recv,
-    pc_send, pc_recv, ring_send, ring_recv, oy_send, oy_recv, gy_send, gy_recv, gz_send, gz_recv,
+    relay, local_sem, qy_send, qy_recv, ky_send, ky_recv, p_send, p_recv, px_send, px_recv,
+    pc_send, pc_recv, ring_send, ring_recv, oy_send, oy_recv, g_send, g_recv,
 ):
     r = lax.axis_index("resp")
     s = lax.axis_index("seq")
@@ -82,9 +85,15 @@
     for copy in own:
         copy.start()
     barrier = pltpu.get_barrier_semaphore()
-    peers = [ahead(d) for d in range(1, NY)] + [along(d) for d in range(1, NZ)] + [across(d) for d in range(1, NX)] + [twin]
-    for peer in peers:
+    others = [across(d) for d in range(1, NX)] + [twin]
+    for peer in others:
         pl.semaphore_signal(barrier, inc=1, device_id=peer, device_id_type=MESH)
+
+    def greet(k, carry):
+        pl.semaphore_signal(barrier, inc=1, device_id=(r, lax.rem(s + k, SEQ)), device_id_type=MESH)
+        return carry
+
+    lax.fori_loop(1, SEQ, greet, 0)
 
     for h in range(HEADS):
         cols = slice(h * D, (h + 1) * D)
@@ -104,13 +113,46 @@
         return carry
 
     lax.fori_loop(0, ROWS, pick, 0)
-    pl.semaphore_wait(barrier, len(peers))
+    length = lengths_ref[0]
+    lanes = lax.broadcasted_iota(jnp.int32, (1, ROWS), 1)
+    sub = lax.broadcasted_iota(jnp.int32, (ROWS, ROWS), 0)
+    lane = lax.broadcasted_iota(jnp.int32, (ROWS, ROWS), 1)
+    as_row = lambda column, shift=0: jnp.sum(jnp.where(sub == lane + shift, column, 0.0), axis=0, keepdims=True)
+    as_column = lambda row: jnp.sum(jnp.where(sub == lane, row, 0), axis=1, keepdims=True)
+    place = s * ROWS + lanes
+    live = place < length
+    spot = as_column(ids_ref[...] % D)
+    reference = as_row(jnp.sum(jnp.where(lane == spot, picked[...], 0.0), axis=1, keepdims=True))
+    rewards = jnp.where(live, -KL_BETA * (logp_ref[...] - reference), 0.0)
+    rewards = rewards + jnp.where(place == length - 1, scores_ref[0], 0.0)
+    rate = -1.0 / jnp.full((1, 1), horizon_ref[0], F32)
+    gamma = jnp.exp(lanes.astype(F32) * rate)
+    pl.semaphore_wait(barrier, len(others) + SEQ - 1)
 
     sent = []
-    p_y, k_y, q_y = [], [], {}
-    for d in range(1, NY):
-        to = lax.rem(y + d, NY)
-        p_y.append(remote(pkv.at[to], pg.at[x, c, z, y], py_send.at[d - 1], py_recv.at[d - 1], ahead(d)))
+
+    def prompt_copy(k):
+        to = lax.rem(s + k, SEQ)
+        return pltpu.make_async_remote_copy(
+            src_ref=pkv.at[to // NZ], dst_ref=pg.at[x, c, z, y], send_sem=p_send.at[k - 1], recv_sem=p_recv.at[k - 1],
+            device_id=(r, to), device_id_type=MESH,
+        )
+
+    def packet_copy(k):
+        return pltpu.make_async_remote_copy(
+            src_ref=packet, dst_ref=packets.at[z, y], send_sem=g_send.at[k - 1], recv_sem=g_recv.at[k - 1],
+            device_id=(r, lax.rem(s + k, SEQ)), device_id_type=MESH,
+        )
+
+    def to_all(act):
+        def step(k, carry):
+            act(k)
+            return carry
+
+        lax.fori_loop(1, SEQ, step, 0)
+
+    to_all(lambda k: prompt_copy(k).start())
+    k_y, q_y = [], {}
     for d in range(1, NY):
         to = lax.rem(y + d, NY)
         for i, src in enumerate((k_hbm, v_hbm)):
@@ -120,15 +162,17 @@
                     ky_send.at[d - 1, i], ky_recv.at[d - 1, i], ahead(d),
                 )
             )
-    for d in (1, 3, 2):
+
+    def send_queries(d):
         to = lax.rem(y + d, NY)
         q_y[d] = remote(q_hbm.at[0, :, head_cols(to, STACK)], qg.at[y], qy_send.at[d - 1], qy_recv.at[d - 1], ahead(d))
-    sent += p_y + k_y + list(q_y.values())
-
-    for copy in p_y:
-        copy.wait_recv()
-    p_z = [remote(pg.at[x, c, z], pg.at[x, c, z], pz_send.at[d - 1], pz_recv.at[d - 1], along(d)) for d in range(1, NZ)]
-    sent += p_z
+
+    send_queries(1)
+    send_queries(3)
+
+    to_all(lambda k: prompt_copy(k).wait_recv())
+    p_x = {d: remote(pg.at[x, c], pg.at[x, c], px_send.at[d - 1], px_recv.at[d - 1], across(d)) for d in (1, 3)}
+    p_c = {0: remote(pg.at[x, c], pg.at[x, c], pc_send.at[0], pc_recv.at[0], twin)}
     for copy in own[1:3]:
         copy.wait()
     for copy in k_y:
@@ -149,68 +193,77 @@
         return out
 
     ring = ring_step(0)
-    for copy in p_z:
-        copy.wait_recv()
-    p_x = {d: remote(pg.at[x, c], pg.at[x, c], px_send.at[d - 1], px_recv.at[d - 1], across(d)) for d in (1, 3, 2)}
-    p_c = {0: remote(pg.at[x, c], pg.at[x, c], pc_send.at[0], pc_recv.at[0], twin)}
 
     def pass_over(d):
-        p_x[d].wait_recv()
         src = lax.rem(x - d + NX, NX)
         p_c[d] = remote(pg.at[src, c], pg.at[src, c], pc_send.at[d], pc_recv.at[d], twin)
 
-    def unpack(i, d):
-        p_c[d].wait_recv()
-        both = pg[lax.rem(x - d + NX, NX)].astype(F32).reshape(2 * NZ * NY, 16, D)
-        pk_all[i] = both[:, :8, :].reshape(CHUNK, D).astype(BF16)
-        pv_all[i] = both[:, 8:, :].reshape(CHUNK, D).astype(BF16)
-
-    def prompt_fold(i, d):
+    def unpack(chunk, half, d, core):
+        both = pg[lax.rem(x - d + NX, NX), core].astype(F32).reshape(SEQ, 16, D)
+        rows = slice(half * SHARE, (half + 1) * SHARE)
+        pk_all[chunk, rows] = both[:, :8, :].reshape(SHARE, D).astype(BF16)
+        pv_all[chunk, rows] = both[:, 8:, :].reshape(SHARE, D).astype(BF16)
+
+    def prompt_fold(i, d, rows=slice(None), first=False):
         block = lax.rem(y - d + NY, NY)
-        if i == 0:
-            if d == 0:
-                own[0].wait()
-            else:
-                q_y[d].wait_recv()
+        if first:
             state = (jnp.full((STACK, D), NEG, F32), jnp.zeros((STACK, D), F32), jnp.zeros((STACK, D), F32))
         else:
             state = (peak[block], total[block], acc[block])
-        peak[block], total[block], acc[block] = fold(state, stacked(qg, block), pk_all[i], pv_all[i])
+        peak[block], total[block], acc[block] = fold(state, stacked(qg, block), pk_all[i, rows], pv_all[i, rows])
 
     def ring_on(step):
         for copy in ring:
             copy.wait_recv()
         return ring_step(step)
 
-    unpack(0, 0)
-    prompt_fold(0, 0)
-    pass_over(1)
-    prompt_fold(0, 1)
-    pass_over(3)
-    prompt_fold(0, 3)
+    near = (0, 1, 3)
+    unpack(0, 0, 0, c)
+    for d in near:
+        if d == 0:
+            own[0].wait()
+        else:
+            q_y[d].wait_recv()
+        prompt_fold(0, d, slice(0, SHARE), True)
+    send_queries(2)
+    p_c[0].wait_recv()
+    unpack(0, 1, 0, 1 - c)
+    for d in near:
+        prompt_fold(0, d, slice(SHARE, 2 * SHARE))
+    for d in (1, 3):
+        p_x[d].wait_recv()
+    for d in (1, 3):
+        pass_over(d)
+    way = 1 + 2 * c
+    relayed = lax.rem(x - way + NX, NX)
+    p_x[2] = remote(pg.at[relayed, c], pg.at[relayed, c], px_send.at[1], px_recv.at[1], across(way))
+    unpack(1, 0, 1, c)
+    unpack(1, 1, 3, c)
+    for d in near:
+        prompt_fold(1, d)
     ring = ring_on(1)
+    for d in (1, 3):
+        p_c[d].wait_recv()
+    unpack(2, 0, 1, 1 - c)
+    unpack(2, 1, 3, 1 - c)
+    prompt_fold(2, 0)
+    p_x[2].wait_recv()
     pass_over(2)
-    unpack(1, 1)
-    for d in (0, 1, 3):
-        prompt_fold(1, d)
-    unpack(2, 3)
-    prompt_fold(2, 0)
-    ring = ring_on(2)
     for d in (1, 3):
         prompt_fold(2, d)
-    for i in range(3):
-        prompt_fold(i, 2)
-    ring = ring_on(3)
-    unpack(3, 2)
-    for d in (0, 1, 3, 2):
+    p_c[2].wait_recv()
+    unpack(3, 0, 2, c)
+    unpack(3, 1, 2, 1 - c)
+    for d in near:
         prompt_fold(3, d)
-    sent += list(p_x.values()) + list(p_c.values())
-
-    length = lengths_ref[0]
-    lanes = lax.broadcasted_iota(jnp.int32, (1, ROWS), 1)
+    ring = ring_on(2)
+    q_y[2].wait_recv()
+    for i in range(PROMPT // CHUNK):
+        prompt_fold(i, 2, first=i == 0)
+    sent += k_y + list(q_y.values()) + list(p_x.values()) + list(p_c.values())
 
     def turn(t):
-        return lax.rem(2 + 3 * t + 3 * (t * (t - 1) // 2), NY)
+        return lax.rem(2 + t + t * (t - 1) // 2, NY)
 
     def reply_half(half):
         for sup in range(NY):
@@ -230,21 +283,59 @@
             peak[block], total[block], acc[block] = state
 
         def step(t, carry):
-            d = turn(t)
-            block = lax.rem(y + d, NY)
+            block = lax.rem(y + turn(t), NY)
+            if half == 0:
+
+                @pl.when(t == 2)
+                def _():
+                    for copy in ring:
+                        copy.wait_recv()
+                    for copy in last_step():
+                        copy.start()
+
             lax.switch(block, [functools.partial(run, b) for b in range(NY)])
             if half == 1:
                 out = (acc[block] / total[block]).astype(BF16)
+                part = jnp.zeros((ROWS, D), F32)
                 for j in range(GROUP):
-                    ob[t, :, j * D : (j + 1) * D] = out[j * ROWS : (j + 1) * ROWS]
-
-                @pl.when(t < NY - 1)
+                    mine = out[j * ROWS : (j + 1) * ROWS]
+                    ob[t, :, j * D : (j + 1) * D] = mine
+                    part = part + mine.astype(F32) * head_ref[y, j : j + 1, :]
+
+                @pl.when(t == 0)
+                def _():
+                    for copy in far_home():
+                        copy.start()
+
+                @pl.when((t > 0) & (t < NY - 1))
                 def _():
                     home(t).start()
 
+                @pl.when(t == 2)
+                def _():
+                    far_home()[1].wait_recv()
+                    relay_home().start()
+
+                here = (block * NZ + z) * ROWS + lax.broadcasted_iota(jnp.int32, (ROWS, 1), 0)
+                column = jnp.where(here < length, jnp.sum(part, axis=1, keepdims=True), 0.0)
+                row = as_row(column)
+                change = jnp.where((block * NZ + z) * ROWS + lanes < length, as_row(column, 1) - row, 0.0)
+                change = change + jnp.where(block == y, rewards, 0.0)
+                lead = jnp.sum(change * gamma, axis=1, keepdims=True)
+                packet[pl.ds(block, 1), :] = jnp.where(lanes == 0, lead, jnp.where(lanes == 1, row[:, :1], 0.0))
             return carry
 
         lax.fori_loop(0, NY, step, 0)
+
+    def last_step():
+        back, fore = lax.rem(z + NZ - 3, NZ), lax.rem(z + 3, NZ)
+        return [
+            pltpu.make_async_remote_copy(
+                src_ref=ref, dst_ref=ref, send_sem=ring_send.at[3, i], recv_sem=ring_recv.at[3, i],
+                device_id=along(d), device_id_type=MESH,
+            )
+            for i, (ref, d) in enumerate(((kvg.at[0, :, back], 1), (kvg.at[1, :, fore], NZ - 1)))
+        ]
 
     def home(t):
         return pltpu.make_async_remote_copy(
@@ -252,14 +343,33 @@
             device_id=ahead(turn(t)), device_id_type=MESH,
         )
 
+    def far_home():
+        return [
+            pltpu.make_async_remote_copy(
+                src_ref=ob.at[0, :, :WING], dst_ref=og.at[y, :, :WING], send_sem=oy_send.at[0], recv_sem=oy_recv.at[0],
+                device_id=ahead(2), device_id_type=MESH,
+            ),
+            pltpu.make_async_remote_copy(
+                src_ref=ob.at[0, :, WING:], dst_ref=relay, send_sem=oy_send.at[3], recv_sem=oy_recv.at[3],
+                device_id=ahead(3), device_id_type=MESH,
+            ),
+        ]
+
+    def relay_home():
+        return pltpu.make_async_remote_copy(
+            src_ref=relay, dst_ref=og.at[lax.rem(y + 1, NY), :, WING:], send_sem=oy_send.at[4], recv_sem=oy_recv.at[4],
+            device_id=ahead(3), device_id_type=MESH,
+        )
+
+    packet[...] = jnp.zeros_like(packet)
     reply_half(0)
-    for copy in ring:
+    for copy in last_step():
         copy.wait_recv()
     reply_half(1)
+    packets[z, y] = packet[...]
+    to_all(lambda k: packet_copy(k).start())
     og[y] = ob[NY - 1]
-    o_y = [home(t) for t in range(NY - 1)]
-    sent += o_y
-    for copy in o_y:
+    for copy in (home(1), home(2), far_home()[0], relay_home()):
         copy.wait_recv()
     back_home = [
         pltpu.make_async_copy(og.at[h], attn_ref.at[0, :, h * STACK : (h + 1) * STACK], local_sem.at[4 + h])
@@ -268,56 +378,40 @@
     for copy in back_home:
         copy.start()
 
-    value = jnp.zeros((ROWS, 1), F32)
+    value = jnp.zeros((ROWS, D), F32)
     for h in range(HEADS):
-        value = value + jnp.sum(og[h].astype(F32) * head_ref[:, h * STACK : (h + 1) * STACK], axis=1, keepdims=True)
-    sub = lax.broadcasted_iota(jnp.int32, (ROWS, ROWS), 0)
-    lane = lax.broadcasted_iota(jnp.int32, (ROWS, ROWS), 1)
-    as_row = lambda column, shift=0: jnp.sum(jnp.where(sub == lane + shift, column, 0.0), axis=0, keepdims=True)
-    as_column = lambda row: jnp.sum(jnp.where(sub == lane, row, 0), axis=1, keepdims=True)
-    place = s * ROWS + lax.broadcasted_iota(jnp.int32, (1, ROWS), 1)
-    live = place < length
+        for j in range(GROUP):
+            value = value + og[h, :, j * D : (j + 1) * D].astype(F32) * head_ref[h, j : j + 1, :]
+    value = jnp.sum(value, axis=1, keepdims=True)
     value = jnp.where(s * ROWS + lax.broadcasted_iota(jnp.int32, (ROWS, 1), 0) < length, value, 0.0)
     value_row = as_row(value)
     values_ref[...] = value_row
-    spot = as_column(ids_ref[...] % D)
-    reference = as_row(jnp.sum(jnp.where(lane == spot, picked[...], 0.0), axis=1, keepdims=True))
-    rewards = jnp.where(live, -KL_BETA * (logp_ref[...] - reference), 0.0)
-    rewards = rewards + jnp.where(place == length - 1, scores_ref[0], 0.0)
     deltas = jnp.where(live, rewards + as_row(value, 1) - value_row, 0.0)
-    rate = -1.0 / jnp.full((1, 1), horizon_ref[0], F32)
     gap = (lane - sub).astype(F32)
     decay = jnp.where(gap >= 0.0, jnp.exp(jnp.maximum(gap, 0.0) * rate), 0.0)
     local_adv = as_row(jnp.sum(decay * deltas, axis=1, keepdims=True))
-    first = lax.broadcasted_iota(jnp.int32, (8, ROWS), 1)
-    packet[...] = jnp.where(first == 0, local_adv[:, :1], jnp.where(first == 1, value_row[:, :1], 0.0))
-    packets[z, y] = packet[...]
-
-    g_y = [remote(packet, packets.at[z, y], gy_send.at[d - 1], gy_recv.at[d - 1], ahead(d)) for d in range(1, NY)]
-    for copy in g_y:
-        copy.wait_recv()
-    g_z = [remote(packets.at[z], packets.at[z], gz_send.at[d - 1], gz_recv.at[d - 1], along(d)) for d in range(1, NZ)]
-    for copy in g_z:
-        copy.wait_recv()
-    sent += g_y + g_z
+    to_all(lambda k: packet_copy(k).wait_recv())
 
     carry = jnp.zeros((1, 1), F32)
     beyond = jnp.zeros((1, 1), F32)
+    heads = packets[:, 0] + packets[:, 1] + packets[:, 2] + packets[:, 3]
     for yy in range(NY):
-        rows = packets[:, yy, 0, :]
+        rows = heads[:, yy, :]
         far = (yy * NZ + lax.broadcasted_iota(jnp.int32, (NZ, 1), 0) - s - 1).astype(F32)
         adv_weight = jnp.where(far >= 0.0, jnp.exp(jnp.maximum(far, 0.0) * ROWS * rate), 0.0)
         value_weight = jnp.where(far >= 1.0, jnp.exp((jnp.maximum(far - 1.0, 0.0) * ROWS + (ROWS - 1)) * rate), 0.0)
         carry = carry + jnp.sum(adv_weight * rows[:, :1] + value_weight * rows[:, 1:2], axis=0, keepdims=True)
         beyond = beyond + jnp.sum(jnp.where(far == 0.0, rows[:, 1:2], 0.0), axis=0, keepdims=True)
-    along_row = lax.broadcasted_iota(jnp.int32, (1, ROWS), 1).astype(F32)
+    along_row = lanes.astype(F32)
     tail = jnp.exp((ROWS - 1 - along_row) * rate) * beyond + jnp.exp((ROWS - along_row) * rate) * carry
     adv_ref[...] = jnp.where(live, local_adv + tail, 0.0)
 
     for copy in back_home:
         copy.wait()
-    for copy in sent:
+    for copy in sent + last_step() + far_home() + [relay_home(), home(1), home(2)]:
         copy.wait_send()
+    to_all(lambda k: prompt_copy(k).wait_send())
+    to_all(lambda k: packet_copy(k).wait_send())
 
 
 def local(queries, resp_keys, response_values, prompt_keys, prompt_values, value_head, token_ids, logprobs, ref_table, scores, lengths, horizon):
@@ -353,24 +447,23 @@
             pltpu.VMEM((ROWS, D), F32),
             pltpu.VMEM((8, ROWS), F32),
             pltpu.VMEM((NZ, NY, 8, ROWS), F32),
+            pltpu.VMEM((ROWS, WING), BF16),
             dma((8,)),
             dma((NY - 1,)), dma((NY - 1,)),
             dma((NY - 1, 2)), dma((NY - 1, 2)),
-            dma((NY - 1,)), dma((NY - 1,)),
-            dma((NZ - 1,)), dma((NZ - 1,)),
+            dma((SEQ - 1,)), dma((SEQ - 1,)),
             dma((NX - 1,)), dma((NX - 1,)),
             dma((NX,)), dma((NX,)),
             dma((NZ // 2, 2)), dma((NZ // 2, 2)),
-            dma((NY - 1,)), dma((NY - 1,)),
-            dma((NY - 1,)), dma((NY - 1,)),
-            dma((NZ - 1,)), dma((NZ - 1,)),
+            dma((5,)), dma((5,)),
+            dma((SEQ - 1,)), dma((SEQ - 1,)),
         ],
         compiler_params=pltpu.CompilerParams(
             collective_id=0, has_side_effects=True, vmem_limit_bytes=56 * 2**20
         ),
     )(
         scores, lengths, horizon, token_ids, queries, resp_keys, response_values, prompt_keys, prompt_values,
-        value_head.reshape(1, HEADS * STACK), token_ids, logprobs, ref_table.reshape(VOCAB // D, D),
+        value_head.reshape(HEADS, GROUP, D), token_ids, logprobs, ref_table.reshape(VOCAB // D, D),
     )
 
 

time: 85.8 us -> 80 us (0.932)
  Pallas kernels: 78.9 us -> 73.8 us
    pallas_call x1, Pallas kernels: 78.9 us -> 73.8 us  [local(): pl.pallas_call(body, out_shape=(jax.ShapeDtypeStruct((1, ROWS, HEADS * ST...]
where the time goes in v1:
time: 80 us; the launch traced here: 79.8 us
  Pallas kernels  73.8 us (92%)
  local copies, waits for them, and re-layouts  3.38 us (4%)
  between operations  2.59 us (3%)
    pallas_call x1, Pallas kernels, local(): pl.pallas_call(body, out_shape=(jax.ShapeDtypeStruct((1, ROWS, HEADS * ST...  73.8 us
    unnamed x7, local copies, waits for them, and re-layouts  3.38 us

profile of v1, /device:TPU:8, one launch (start us, length us, event | category | flops | bytes accessed | tf_op | source)
XLA Modules:
  0.0 79.8 jit_solution(2613318221440697574)
XLA Ops:
  2.6 73.8 %shard_map.139 = (bf16[1,128,4096]{2,1,0:T(8,128)(2,1)}, f32[1,128]{1,0:T(1,128)}, f32[1,128]{1,0:T(1,128)}) custom-call(f32[1]{0:T(128)S(6)} %copy.18.scores_ref, s32[1]{0:T(128)S(6)} %copy.19.lengths_ref, f32[1]{0:T(128)S(6)} %copy.20.horizon_ref, s32[1,128]{1,0:T(1,128)} %ids_ref.1, bf16[1,128,4096]{2,1,0:T(8,128)(2,1)} %q_hbm.1, ...), custom_call_target="tpu_custom_call" | custom-call | tf_op jit(solution)/shard_map/pallas_call | solution.py:422
  76.4 0.0 copy-start.1
  76.4 2.3 %copy.21 = bf16[1,128,4096]{2,1,0:T(8,128)(2,1)} copy(bf16[1,128,4096]{2,1,0:T(8,128)(2,1)} %get-tuple-element.6) | data formatting | bytes 2097152
  78.7 0.0 copy-done.1
  78.7 0.0 copy-start
  78.7 0.5 copy.22
  79.2 0.1 copy-done
  79.3 0.5 copy.23
Async XLA Ops:
  76.4 2.3 %copy-start.1 = (f32[1,128]{1,0:T(1,128)S(1)}, f32[1,128]{1,0:T(1,128)}, u32[]{:S(2)}) copy-start(f32[1,128]{1,0:T(1,128)} %get-tuple-element.7) | copy-start | bytes 1540
  78.7 0.6 copy-start

commit v2 on v1

--- a/solution.py
+++ b/solution.py
@@ -38,9 +38,8 @@
     if bias is not None:
         s = (s.reshape(GROUP, ROWS, -1) + bias[None]).reshape(s.shape)
     new = jnp.maximum(peak, jnp.max(s, axis=1, keepdims=True))
-    scaled = new * SCALE
-    w = jnp.exp2(s * SCALE - jnp.concatenate([scaled] * (s.shape[1] // D), axis=1))
-    shrink = jnp.exp2(peak * SCALE - scaled)
+    w = jnp.exp2((s - jnp.concatenate([new] * (s.shape[1] // D), axis=1)) * SCALE)
+    shrink = jnp.exp2((peak - new) * SCALE)
     total = total * shrink + jnp.sum(w, axis=1, keepdims=True)
     acc = acc * shrink + jnp.dot(w.astype(BF16), v, preferred_element_type=F32)
     return new, total, acc
@@ -54,7 +53,7 @@
     scores_ref, lengths_ref, horizon_ref, ids_smem, q_hbm, k_hbm, v_hbm, pk_ref, pv_ref, head_ref, ids_ref, logp_ref, table_hbm,
     attn_ref, values_ref, adv_ref,
     qg, kvg, pkv, pg, pk_all, pv_all, acc, peak, total, staged, past, causal, ob, og, table, picked, packet, packets,
-    relay, local_sem, qy_send, qy_recv, ky_send, ky_recv, p_send, p_recv, px_send, px_recv,
+    relay, spare_p, spare_g, local_sem, qy_send, qy_recv, ky_send, ky_recv, p_send, p_recv, px_send, px_recv,
     pc_send, pc_recv, ring_send, ring_recv, oy_send, oy_recv, g_send, g_recv,
 ):
     r = lax.axis_index("resp")
@@ -98,7 +97,51 @@
     for h in range(HEADS):
         cols = slice(h * D, (h + 1) * D)
         pkv[h] = jnp.concatenate([pk_ref[:, cols].astype(F32), pv_ref[:, cols].astype(F32)], axis=0).astype(BF16)
-    pg[x, c, z, y] = pkv[y]
+
+    pl.semaphore_wait(barrier, len(others) + SEQ - 1)
+
+    sent = []
+
+    def prompt_copy(k):
+        to = lax.rem(s + k, SEQ)
+        return pltpu.make_async_remote_copy(
+            src_ref=pkv.at[to // NZ], dst_ref=pg.at[x, c, z, y], send_sem=p_send, recv_sem=p_recv,
+            device_id=(r, to), device_id_type=MESH,
+        )
+
+    def packet_copy(k):
+        return pltpu.make_async_remote_copy(
+            src_ref=packet, dst_ref=packets.at[z, y], send_sem=g_send, recv_sem=g_recv,
+            device_id=(r, lax.rem(s + k, SEQ)), device_id_type=MESH,
+        )
+
+    def to_all(act):
+        def step(k, carry):
+            act(k)
+            return carry
+
+        lax.fori_loop(1, SEQ, step, 0)
+
+    to_all(lambda k: prompt_copy(k).start())
+    pltpu.make_async_copy(pkv.at[y], pg.at[x, c, z, y], p_recv).start()
+    pltpu.make_async_copy(pkv.at[y], spare_p.at[z, y], p_send).start()
+    k_y, q_y = [], {}
+    for d in range(1, NY):
+        to = lax.rem(y + d, NY)
+        for i, src in enumerate((k_hbm, v_hbm)):
+            k_y.append(
+                remote(
+                    src.at[0, :, head_cols(to, D)], kvg.at[i, y, z],
+                    ky_send.at[d - 1, i], ky_recv.at[d - 1, i], ahead(d),
+                )
+            )
+
+    def send_queries(d):
+        to = lax.rem(y + d, NY)
+        q_y[d] = remote(q_hbm.at[0, :, head_cols(to, STACK)], qg.at[y], qy_send.at[d - 1], qy_recv.at[d - 1], ahead(d))
+
+    send_queries(1)
+    send_queries(3)
 
     order = [lax.rem(z + k + NZ, NZ) for k in (0, 1, -1, 2, -2, 3, -3, 4)]
     inside = lax.broadcasted_iota(jnp.int32, (ROWS, ROWS), 1) - lax.broadcasted_iota(jnp.int32, (ROWS, ROWS), 0)
@@ -127,50 +170,7 @@
     rewards = rewards + jnp.where(place == length - 1, scores_ref[0], 0.0)
     rate = -1.0 / jnp.full((1, 1), horizon_ref[0], F32)
     gamma = jnp.exp(lanes.astype(F32) * rate)
-    pl.semaphore_wait(barrier, len(others) + SEQ - 1)
-
-    sent = []
-
-    def prompt_copy(k):
-        to = lax.rem(s + k, SEQ)
-        return pltpu.make_async_remote_copy(
-            src_ref=pkv.at[to // NZ], dst_ref=pg.at[x, c, z, y], send_sem=p_send.at[k - 1], recv_sem=p_recv.at[k - 1],
-            device_id=(r, to), device_id_type=MESH,
-        )
-
-    def packet_copy(k):
-        return pltpu.make_async_remote_copy(
-            src_ref=packet, dst_ref=packets.at[z, y], send_sem=g_send.at[k - 1], recv_sem=g_recv.at[k - 1],
-            device_id=(r, lax.rem(s + k, SEQ)), device_id_type=MESH,
-        )
-
-    def to_all(act):
-        def step(k, carry):
-            act(k)
-            return carry
-
-        lax.fori_loop(1, SEQ, step, 0)
-
-    to_all(lambda k: prompt_copy(k).start())
-    k_y, q_y = [], {}
-    for d in range(1, NY):
-        to = lax.rem(y + d, NY)
-        for i, src in enumerate((k_hbm, v_hbm)):
-            k_y.append(
-                remote(
-                    src.at[0, :, head_cols(to, D)], kvg.at[i, y, z],
-                    ky_send.at[d - 1, i], ky_recv.at[d - 1, i], ahead(d),
-                )
-            )
-
-    def send_queries(d):
-        to = lax.rem(y + d, NY)
-        q_y[d] = remote(q_hbm.at[0, :, head_cols(to, STACK)], qg.at[y], qy_send.at[d - 1], qy_recv.at[d - 1], ahead(d))
-
-    send_queries(1)
-    send_queries(3)
-
-    to_all(lambda k: prompt_copy(k).wait_recv())
+    pltpu.make_async_copy(spare_p, pg.at[x, c], p_recv).wait()
     p_x = {d: remote(pg.at[x, c], pg.at[x, c], px_send.at[d - 1], px_recv.at[d - 1], across(d)) for d in (1, 3)}
     p_c = {0: remote(pg.at[x, c], pg.at[x, c], pc_send.at[0], pc_recv.at[0], twin)}
     for copy in own[1:3]:
@@ -366,8 +366,9 @@
     for copy in last_step():
         copy.wait_recv()
     reply_half(1)
-    packets[z, y] = packet[...]
     to_all(lambda k: packet_copy(k).start())
+    pltpu.make_async_copy(packet, packets.at[z, y], g_recv).start()
+    pltpu.make_async_copy(packet, spare_g.at[z, y], g_send).start()
     og[y] = ob[NY - 1]
     for copy in (home(1), home(2), far_home()[0], relay_home()):
         copy.wait_recv()
@@ -390,7 +391,7 @@
     gap = (lane - sub).astype(F32)
     decay = jnp.where(gap >= 0.0, jnp.exp(jnp.maximum(gap, 0.0) * rate), 0.0)
     local_adv = as_row(jnp.sum(decay * deltas, axis=1, keepdims=True))
-    to_all(lambda k: packet_copy(k).wait_recv())
+    pltpu.make_async_copy(spare_g, packets, g_recv).wait()
 
     carry = jnp.zeros((1, 1), F32)
     beyond = jnp.zeros((1, 1), F32)
@@ -410,8 +411,8 @@
         copy.wait()
     for copy in sent + last_step() + far_home() + [relay_home(), home(1), home(2)]:
         copy.wait_send()
-    to_all(lambda k: prompt_copy(k).wait_send())
-    to_all(lambda k: packet_copy(k).wait_send())
+    pltpu.make_async_copy(pg.at[x, c], spare_p, p_send).wait()
+    pltpu.make_async_copy(packets, spare_g, g_send).wait()
 
 
 def local(queries, resp_keys, response_values, prompt_keys, prompt_values, value_head, token_ids, logprobs, ref_table, scores, lengths, horizon):
@@ -448,15 +449,17 @@
             pltpu.VMEM((8, ROWS), F32),
             pltpu.VMEM((NZ, NY, 8, ROWS), F32),
             pltpu.VMEM((ROWS, WING), BF16),
+            pltpu.VMEM((NZ, NY, 16, D), BF16),
+            pltpu.VMEM((NZ, NY, 8, ROWS), F32),
             dma((8,)),
             dma((NY - 1,)), dma((NY - 1,)),
             dma((NY - 1, 2)), dma((NY - 1, 2)),
-            dma((SEQ - 1,)), dma((SEQ - 1,)),
+            dma, dma,
             dma((NX - 1,)), dma((NX - 1,)),
             dma((NX,)), dma((NX,)),
             dma((NZ // 2, 2)), dma((NZ // 2, 2)),
             dma((5,)), dma((5,)),
-            dma((SEQ - 1,)), dma((SEQ - 1,)),
+            dma, dma,
         ],
         compiler_params=pltpu.CompilerParams(
             collective_id=0, has_side_effects=True, vmem_limit_bytes=56 * 2**20

time: 80 us -> 76.8 us (0.960)
  Pallas kernels: 73.8 us -> 70.6 us
    pallas_call x1, Pallas kernels: 73.8 us -> 70.6 us  [local(): pl.pallas_call(body, out_shape=(jax.ShapeDtypeStruct((1, ROWS, HEADS * ST...]
where the time goes in v2:
time: 76.8 us; the launch traced here: 76.6 us
  Pallas kernels  70.6 us (92%)
  local copies, waits for them, and re-layouts  3.38 us (4%)
  between operations  2.59 us (3%)
    pallas_call x1, Pallas kernels, local(): pl.pallas_call(body, out_shape=(jax.ShapeDtypeStruct((1, ROWS, HEADS * ST...  70.6 us
    unnamed x7, local copies, waits for them, and re-layouts  3.38 us

profile of v2, /device:TPU:8, one launch (start us, length us, event | category | flops | bytes accessed | tf_op | source)
XLA Modules:
  0.0 76.6 jit_solution(2529874590445996222)
XLA Ops:
  2.6 70.6 %shard_map.139 = (bf16[1,128,4096]{2,1,0:T(8,128)(2,1)}, f32[1,128]{1,0:T(1,128)}, f32[1,128]{1,0:T(1,128)}) custom-call(f32[1]{0:T(128)S(6)} %copy.18.scores_ref, s32[1]{0:T(128)S(6)} %copy.19.lengths_ref, f32[1]{0:T(128)S(6)} %copy.20.horizon_ref, s32[1,128]{1,0:T(1,128)} %ids_ref.1, bf16[1,128,4096]{2,1,0:T(8,128)(2,1)} %q_hbm.1, ...), custom_call_target="tpu_custom_call" | custom-call | tf_op jit(solution)/shard_map/pallas_call | solution.py:423
  73.2 0.0 copy-start.1
  73.2 2.3 %copy.21 = bf16[1,128,4096]{2,1,0:T(8,128)(2,1)} copy(bf16[1,128,4096]{2,1,0:T(8,128)(2,1)} %get-tuple-element.6) | data formatting | bytes 2097152
  75.5 0.0 copy-done.1
  75.5 0.0 copy-start
  75.5 0.5 copy.22
  76.0 0.1 copy-done
  76.0 0.5 copy.23
Async XLA Ops:
  73.2 2.3 %copy-start.1 = (f32[1,128]{1,0:T(1,128)S(1)}, f32[1,128]{1,0:T(1,128)}, u32[]{:S(2)}) copy-start(f32[1,128]{1,0:T(1,128)} %get-tuple-element.7) | copy-start | bytes 1540
  75.5 0.6 copy-start

commit v3 on v2

--- a/solution.py
+++ b/solution.py
@@ -51,7 +51,7 @@
 
 def body(
     scores_ref, lengths_ref, horizon_ref, ids_smem, q_hbm, k_hbm, v_hbm, pk_ref, pv_ref, head_ref, ids_ref, logp_ref, table_hbm,
-    attn_ref, values_ref, adv_ref,
+    heads_ref, values_ref, adv_ref,
     qg, kvg, pkv, pg, pk_all, pv_all, acc, peak, total, staged, past, causal, ob, og, table, picked, packet, packets,
     relay, spare_p, spare_g, local_sem, qy_send, qy_recv, ky_send, ky_recv, p_send, p_recv, px_send, px_recv,
     pc_send, pc_recv, ring_send, ring_recv, oy_send, oy_recv, g_send, g_recv,
@@ -204,32 +204,31 @@
         pk_all[chunk, rows] = both[:, :8, :].reshape(SHARE, D).astype(BF16)
         pv_all[chunk, rows] = both[:, 8:, :].reshape(SHARE, D).astype(BF16)
 
-    def prompt_fold(i, d, rows=slice(None), first=False):
+    def prompt_fold(d, *chunks, first=False):
         block = lax.rem(y - d + NY, NY)
         if first:
             state = (jnp.full((STACK, D), NEG, F32), jnp.zeros((STACK, D), F32), jnp.zeros((STACK, D), F32))
         else:
             state = (peak[block], total[block], acc[block])
-        peak[block], total[block], acc[block] = fold(state, stacked(qg, block), pk_all[i, rows], pv_all[i, rows])
+        q = stacked(qg, block)
+        for chunk in chunks:
+            state = fold(state, q, pk_all[chunk], pv_all[chunk])
+        peak[block], total[block], acc[block] = state
 
     def ring_on(step):
         for copy in ring:
             copy.wait_recv()
         return ring_step(step)
 
-    near = (0, 1, 3)
     unpack(0, 0, 0, c)
-    for d in near:
-        if d == 0:
-            own[0].wait()
-        else:
-            q_y[d].wait_recv()
-        prompt_fold(0, d, slice(0, SHARE), True)
-    send_queries(2)
+    own[0].wait()
+    prompt_fold(0, (0, slice(0, SHARE)), first=True)
     p_c[0].wait_recv()
     unpack(0, 1, 0, 1 - c)
-    for d in near:
-        prompt_fold(0, d, slice(SHARE, 2 * SHARE))
+    prompt_fold(0, (0, slice(SHARE, 2 * SHARE)))
+    for d in (1, 3):
+        q_y[d].wait_recv()
+    send_queries(2)
     for d in (1, 3):
         p_x[d].wait_recv()
     for d in (1, 3):
@@ -239,27 +238,26 @@
     p_x[2] = remote(pg.at[relayed, c], pg.at[relayed, c], px_send.at[1], px_recv.at[1], across(way))
     unpack(1, 0, 1, c)
     unpack(1, 1, 3, c)
-    for d in near:
-        prompt_fold(1, d)
+    for d in (1, 3):
+        prompt_fold(d, 0, 1, first=True)
+    p_x[2].wait_recv()
+    pass_over(2)
+    prompt_fold(0, 1)
     ring = ring_on(1)
     for d in (1, 3):
         p_c[d].wait_recv()
     unpack(2, 0, 1, 1 - c)
     unpack(2, 1, 3, 1 - c)
-    prompt_fold(2, 0)
-    p_x[2].wait_recv()
-    pass_over(2)
-    for d in (1, 3):
-        prompt_fold(2, d)
+    prompt_fold(0, 2)
     p_c[2].wait_recv()
     unpack(3, 0, 2, c)
     unpack(3, 1, 2, 1 - c)
-    for d in near:
-        prompt_fold(3, d)
+    for d in (1, 3):
+        prompt_fold(d, 2, 3)
+    prompt_fold(0, 3)
     ring = ring_on(2)
     q_y[2].wait_recv()
-    for i in range(PROMPT // CHUNK):
-        prompt_fold(i, 2, first=i == 0)
+    prompt_fold(2, *range(PROMPT // CHUNK), first=True)
     sent += k_y + list(q_y.values()) + list(p_x.values()) + list(p_c.values())
 
     def turn(t):
@@ -373,7 +371,7 @@
     for copy in (home(1), home(2), far_home()[0], relay_home()):
         copy.wait_recv()
     back_home = [
-        pltpu.make_async_copy(og.at[h], attn_ref.at[0, :, h * STACK : (h + 1) * STACK], local_sem.at[4 + h])
+        pltpu.make_async_copy(og.at[h], heads_ref.at[h], local_sem.at[4 + h])
         for h in range(HEADS)
     ]
     for copy in back_home:
@@ -420,10 +418,10 @@
     vmem = pl.BlockSpec(memory_space=pltpu.VMEM)
     hbm = pl.BlockSpec(memory_space=pl.ANY)
     dma = pltpu.SemaphoreType.DMA
-    return pl.pallas_call(
+    heads, values, advantages = pl.pallas_call(
         body,
         out_shape=(
-            jax.ShapeDtypeStruct((1, ROWS, HEADS * STACK), BF16),
+            jax.ShapeDtypeStruct((HEADS, ROWS, STACK), BF16),
             jax.ShapeDtypeStruct((1, ROWS), F32),
             jax.ShapeDtypeStruct((1, ROWS), F32),
         ),
@@ -468,6 +466,29 @@
         scores, lengths, horizon, token_ids, queries, resp_keys, response_values, prompt_keys, prompt_values,
         value_head.reshape(HEADS, GROUP, D), token_ids, logprobs, ref_table.reshape(VOCAB // D, D),
     )
+    return pl.pallas_call(
+        gather_heads,
+        out_shape=(
+            jax.ShapeDtypeStruct((1, ROWS, HEADS * STACK), BF16),
+            jax.ShapeDtypeStruct((1, ROWS), F32),
+            jax.ShapeDtypeStruct((1, ROWS), F32),
+        ),
+        in_specs=[hbm, vmem, vmem],
+        out_specs=(hbm, vmem, vmem),
+        scratch_shapes=[dma((HEADS,))],
+    )(heads, values, advantages)
+
+
+def gather_heads(heads_ref, values_in, adv_in, attn_ref, values_ref, adv_ref, sem):
+    copies = [
+        pltpu.make_async_copy(heads_ref.at[h], attn_ref.at[0, :, h * STACK : (h + 1) * STACK], sem.at[h]) for h in range(HEADS)
+    ]
+    for copy in copies:
+        copy.start()
+    values_ref[...] = values_in[...]
+    adv_ref[...] = adv_in[...]
+    for copy in copies:
+        copy.wait()
 
 
 def solution(mesh):

time: 76.8 us -> 107 us (1.39)
  Pallas kernels: 70.6 us -> 103 us
  local copies, waits for them, and re-layouts: 3.38 us -> 0 us
    pallas_call x1 -> x2, Pallas kernels: 70.6 us -> 103 us  [the longest x1 69 us: local(): pl.pallas_call(body, out_shape=(jax.ShapeDtypeStruct((HEADS, ROWS, STACK)...]
    unnamed x7 -> x0, local copies, waits for them, and re-layouts: 3.38 us -> none
where the time goes in v3:
time: 107 us; the launch traced here: 106 us
  Pallas kernels  103 us (96%)
  between operations  2.76 us (3%)
    pallas_call x1, Pallas kernels, local(): pl.pallas_call(body, out_shape=(jax.ShapeDtypeStruct((HEADS, ROWS, STACK)...  69 us
    pallas_call x1, Pallas kernels, local(): pl.pallas_call(gather_heads, out_shape=(jax.ShapeDtypeStruct((1, ROWS, HE...  34 us

profile of v3, /device:TPU:8, one launch (start us, length us, event | category | flops | bytes accessed | tf_op | source)
XLA Modules:
  0.0 105.8 jit_solution(15215681826249239304)
XLA Ops:
  2.6 69.0 %shard_map.139 = (bf16[4,128,1024]{2,1,0:T(8,128)(2,1)}, f32[1,128]{1,0:T(1,128)}, f32[1,128]{1,0:T(1,128)}) custom-call(f32[1]{0:T(128)S(6)} %copy.15.scores_ref, s32[1]{0:T(128)S(6)} %copy.16.lengths_ref, f32[1]{0:T(128)S(6)} %copy.17.horizon_ref, s32[1,128]{1,0:T(1,128)} %ids_ref.1, bf16[1,128,4096]{2,1,0:T(8,128)(2,1)} %q_hbm.1, ...), custom_call_target="tpu_custom_call" | custom-call | tf_op jit(solution)/shard_map/pallas_call | solution.py:421
  71.5 34.0 %shard_map.140 = (bf16[1,128,4096]{2,1,0:T(8,128)(2,1)}, f32[1,128]{1,0:T(1,128)}, f32[1,128]{1,0:T(1,128)}) custom-call(bf16[4,128,1024]{2,1,0:T(8,128)(2,1)} %get-tuple-element.6.heads_ref, f32[1,128]{1,0:T(1,128)} %get-tuple-element.7.values_in, f32[1,128]{1,0:T(1,128)} %get-tuple-element.8.adv_in), custom_call_target="tpu_custom_call" | custom-call | tf_op jit(solution)/shard_map/pallas_call | solution.py:469

commit v4 on v3

--- a/solution.py
+++ b/solution.py
@@ -473,22 +473,16 @@
             jax.ShapeDtypeStruct((1, ROWS), F32),
             jax.ShapeDtypeStruct((1, ROWS), F32),
         ),
-        in_specs=[hbm, vmem, vmem],
-        out_specs=(hbm, vmem, vmem),
-        scratch_shapes=[dma((HEADS,))],
+        in_specs=[vmem, vmem, vmem],
+        out_specs=(vmem, vmem, vmem),
     )(heads, values, advantages)
 
 
-def gather_heads(heads_ref, values_in, adv_in, attn_ref, values_ref, adv_ref, sem):
-    copies = [
-        pltpu.make_async_copy(heads_ref.at[h], attn_ref.at[0, :, h * STACK : (h + 1) * STACK], sem.at[h]) for h in range(HEADS)
-    ]
-    for copy in copies:
-        copy.start()
+def gather_heads(heads_ref, values_in, adv_in, attn_ref, values_ref, adv_ref):
+    for h in range(HEADS):
+        attn_ref[0, :, h * STACK : (h + 1) * STACK] = heads_ref[h]
     values_ref[...] = values_in[...]
     adv_ref[...] = adv_in[...]
-    for copy in copies:
-        copy.wait()
 
 
 def solution(mesh):

time: 107 us -> 74.9 us (0.70)
  Pallas kernels: 103 us -> 71.2 us
    pallas_call x1, Pallas kernels: 34 us -> 2.27 us  [local(): pl.pallas_call(gather_heads, out_shape=(jax.ShapeDtypeStruct((1, ROWS, HE...]
where the time goes in v4:
time: 74.9 us; the launch traced here: 73.8 us
  Pallas kernels  71.2 us (95%)
  between operations  2.58 us (3%)
    pallas_call x1, Pallas kernels, local(): pl.pallas_call(body, out_shape=(jax.ShapeDtypeStruct((HEADS, ROWS, STACK)...  69 us
    pallas_call x1, Pallas kernels, local(): pl.pallas_call(gather_heads, out_shape=(jax.ShapeDtypeStruct((1, ROWS, HE...  2.27 us

profile of v4, /device:TPU:8, one launch (start us, length us, event | category | flops | bytes accessed | tf_op | source)
XLA Modules:
  0.0 73.8 jit_solution(1912035130910492883)
XLA Ops:
  2.6 69.0 %shard_map.139 = (bf16[4,128,1024]{2,1,0:T(8,128)(2,1)}, f32[1,128]{1,0:T(1,128)}, f32[1,128]{1,0:T(1,128)}) custom-call(f32[1]{0:T(128)S(6)} %copy.15.scores_ref, s32[1]{0:T(128)S(6)} %copy.16.lengths_ref, f32[1]{0:T(128)S(6)} %copy.17.horizon_ref, s32[1,128]{1,0:T(1,128)} %ids_ref.1, bf16[1,128,4096]{2,1,0:T(8,128)(2,1)} %q_hbm.1, ...), custom_call_target="tpu_custom_call" | custom-call | tf_op jit(solution)/shard_map/pallas_call | solution.py:421
  71.5 2.3 %shard_map.140 = (bf16[1,128,4096]{2,1,0:T(8,128)(2,1)}, f32[1,128]{1,0:T(1,128)}, f32[1,128]{1,0:T(1,128)}) custom-call(bf16[4,128,1024]{2,1,0:T(8,128)(2,1)} %get-tuple-element.6.heads_ref, f32[1,128]{1,0:T(1,128)} %get-tuple-element.7.values_in, f32[1,128]{1,0:T(1,128)} %get-tuple-element.8.adv_in), custom_call_target="tpu_custom_call" | custom-call | tf_op jit(solution)/shard_map/pallas_call | solution.py:469
